TPU v7x, 128 devices: a whole 4x4x4 slice. The times are simulated.
128 devices in a mesh: uly: 8 (over z, x_hi), blk: 16 (over x_lo, y, core).
Axes of the slice: x: 4 (x_hi: 2, x_lo: 2; x = x_hi * 2 + x_lo), y: 4, z: 4, core: 2. Of those that a mesh axis runs over, the one named last changes fastest.
Arguments:
- queries: bfloat16 [1, 12288, 3072], P(None, ('uly', 'blk')), may hold values from -26 to 26
- key_states: bfloat16 [1, 12288, 3072], P(None, ('uly', 'blk')), may hold values from -16 to 16
- value_states: bfloat16 [1, 12288, 3072], P(None, ('uly', 'blk')), may hold values from -6 to 6
Outputs:
- attended: bfloat16 [1, 12288, 3072], P(None, ('uly', 'blk'))
All inputs are finite; a program needn't handle non-finite values.
Results may differ from a plain program's by a relative error of at most 0.0055.
Values may be sent and summed in bfloat16 or wider, within the bound.
No kernel may reach another device: no remote copies, remote signals or barrier semaphores. Data moves between devices by JAX's collectives and lax.ppermute only.
A program may use at most 128 MiB of HBM per device.

v0:
```python
import functools
import math

import jax
import jax.numpy as jnp
from jax import lax
from jax.experimental import pallas as pl
from jax.experimental.pallas import tpu as pltpu
from jax.sharding import Mesh
from jax.sharding import PartitionSpec as P

HEAD = 128
HEADS_HERE = 3
WIDTH = HEAD * HEADS_HERE
GROUPS = 8
TOKENS = 96
ROWS = GROUPS * TOKENS
STAT_ROWS = 32
SENT_ROWS = ROWS + STAT_ROWS
SUB_ROWS = 256
SCALE = math.log2(math.e) / math.sqrt(HEAD)
ULY = ("z", "xh")
VMEM = 20 * 2**20


def regroup_kernel(*refs):
    count = (len(refs) - 2) // 2
    in_refs, out_ref, held, sems = refs[:count], refs[count], refs[count + 1 : -1], refs[-1]
    copies = [
        pltpu.make_async_copy(ref, block, sems.at[part])
        for part, (ref, block) in enumerate(zip(in_refs, held))
    ]
    for copy in copies:
        copy.start()
    for part, (copy, block) in enumerate(zip(copies, held)):
        copy.wait()
        for g in range(GROUPS):
            out_ref[g, :, part * WIDTH : (part + 1) * WIDTH] = block[:, g * WIDTH : (g + 1) * WIDTH]


def regroup(*arrays):
    return pl.pallas_call(
        regroup_kernel,
        in_specs=[pl.BlockSpec(memory_space=pl.ANY)] * len(arrays),
        out_specs=pl.BlockSpec(memory_space=pltpu.VMEM),
        out_shape=jax.ShapeDtypeStruct((GROUPS, TOKENS, len(arrays) * WIDTH), arrays[0].dtype),
        scratch_shapes=[pltpu.VMEM(array.shape, array.dtype) for array in arrays]
        + [pltpu.SemaphoreType.DMA((len(arrays),))],
        compiler_params=pltpu.CompilerParams(vmem_limit_bytes=VMEM),
    )(*arrays)


def copy_out_kernel(in_ref, out_ref, held, sem):
    copy = pltpu.make_async_copy(in_ref, held, sem)
    copy.start()
    copy.wait()
    for g in range(GROUPS):
        for x in range(2):
            out_ref[2 * g + x] = held[:, g * WIDTH : (g + 1) * WIDTH]


def copy_out(queries):
    return pl.pallas_call(
        copy_out_kernel,
        in_specs=[pl.BlockSpec(memory_space=pl.ANY)],
        out_specs=pl.BlockSpec(memory_space=pltpu.VMEM),
        out_shape=jax.ShapeDtypeStruct((2 * GROUPS, TOKENS, WIDTH), queries.dtype),
        scratch_shapes=[pltpu.VMEM(queries.shape, queries.dtype), pltpu.SemaphoreType.DMA],
        compiler_params=pltpu.CompilerParams(vmem_limit_bytes=VMEM),
    )(queries)


def part_kernel(in_ref, own_ref, far_ref):
    own = lax.axis_index("xl")
    for g in range(GROUPS):
        at = slice(g * TOKENS, (g + 1) * TOKENS)
        own_ref[at, :] = in_ref[2 * g + own]
        far_ref[at, :] = in_ref[2 * g + 1 - own]


def part(both):
    whole = pl.BlockSpec(memory_space=pltpu.VMEM)
    return pl.pallas_call(
        part_kernel,
        in_specs=[whole],
        out_specs=[whole, whole],
        out_shape=[jax.ShapeDtypeStruct((ROWS, WIDTH), both.dtype)] * 2,
        compiler_params=pltpu.CompilerParams(vmem_limit_bytes=VMEM),
        cost_estimate=pl.CostEstimate(flops=1, bytes_accessed=1, transcendentals=0),
    )(both)


def ungroup_kernel(in_ref, out_ref):
    for g in range(GROUPS):
        out_ref[:, g * WIDTH : (g + 1) * WIDTH] = in_ref[g]


def ungroup(parts):
    whole = pl.BlockSpec(memory_space=pltpu.VMEM)
    return pl.pallas_call(
        ungroup_kernel,
        in_specs=[whole],
        out_specs=whole,
        out_shape=jax.ShapeDtypeStruct((TOKENS, GROUPS * WIDTH), parts.dtype),
        compiler_params=pltpu.CompilerParams(vmem_limit_bytes=VMEM),
    )(parts)


def diagonal():
    rows = lax.broadcasted_iota(jnp.int32, (HEAD, HEAD), 0)
    cols = lax.broadcasted_iota(jnp.int32, (HEAD, HEAD), 1)
    return rows == cols


def across(column, width):
    return jnp.concatenate([column] * (width // HEAD), axis=1)


def attend_kernel(*refs, places, resumed, final):
    q_ref = refs[0]
    sources = len(places)
    state_ref = refs[-2] if resumed else None
    out_ref = refs[-1]
    tiles = ROWS // SUB_ROWS
    jobs = [(h, t, s) for h in range(HEADS_HERE) for t in range(tiles) for s in range(sources)]
    ones = jnp.ones((ROWS, HEAD), jnp.bfloat16)

    def columns(s, which, h):
        ref, first = places[s][which]
        at = first + h * HEAD
        return refs[ref][:, at : at + HEAD]

    def scores_of(h, t, s):
        return lax.dot_general(
            q_ref[t * SUB_ROWS : (t + 1) * SUB_ROWS, h * HEAD : (h + 1) * HEAD],
            columns(s, 0, h),
            (((1,), (1,)), ((), ())),
            preferred_element_type=jnp.float32,
        )

    top = total = None
    logs = []
    scores = scores_of(*jobs[0])
    for n, (h, t, s) in enumerate(jobs):
        upcoming = scores_of(*jobs[n + 1]) if n + 1 < len(jobs) else None
        at = slice(t * SUB_ROWS, (t + 1) * SUB_ROWS)
        mine = slice(h * HEAD, (h + 1) * HEAD)
        if s == 0 and resumed:
            total = state_ref[h, at, : 2 * HEAD]
            top = state_ref[h, at, 2 * HEAD :]
        first = s == 0 and not resumed
        high = jnp.max(scores, axis=1, keepdims=True) * SCALE
        high = jnp.broadcast_to(high, (SUB_ROWS, HEAD))
        if not first:
            high = jnp.maximum(top, high)
        weights = jnp.exp2(scores * SCALE - across(high, ROWS)).astype(jnp.bfloat16)
        widened = jnp.concatenate([columns(s, 1, h), ones], axis=1)
        product = jnp.dot(weights, widened, preferred_element_type=jnp.float32)
        if not first:
            product = product + total * across(jnp.exp2(top - high), 2 * HEAD)
        top, total = high, product
        if s == sources - 1:
            if final:
                row_sum = total[:, HEAD:]
                out_ref[at, mine] = (total[:, :HEAD] / row_sum).astype(out_ref.dtype)
                logs.append(top + jnp.log2(row_sum))
            else:
                out_ref[h, at, : 2 * HEAD] = total
                out_ref[h, at, 2 * HEAD :] = top
        scores = upcoming
        if final and s == sources - 1 and t == tiles - 1:
            eye = diagonal()
            lines = []
            for log in logs:
                for g in range(SUB_ROWS // HEAD):
                    piece = log[g * HEAD : (g + 1) * HEAD]
                    lines.append(jnp.sum(jnp.where(eye, piece, 0.0), axis=0, keepdims=True))
            lines.append(jnp.zeros((8 - len(lines), HEAD), jnp.float32))
            whole = jnp.concatenate(lines, axis=0)
            part1 = whole.astype(jnp.bfloat16)
            rest = whole - part1.astype(jnp.float32)
            part2 = rest.astype(jnp.bfloat16)
            part3 = (rest - part2.astype(jnp.float32)).astype(jnp.bfloat16)
            out_ref[ROWS:, mine] = jnp.concatenate(
                [part1, part2, part3, jnp.zeros((8, HEAD), jnp.bfloat16)], axis=0
            )
            logs = []


def attend(queries, sources, state=None, final=False):
    whole = pl.BlockSpec(memory_space=pltpu.VMEM)
    operands, places = [queries], []
    for source in sources:
        place = []
        for array, first in (source[:2], source[2:]):
            known = [i for i, operand in enumerate(operands) if operand is array and i > 0]
            if not known:
                operands.append(array)
            place.append((known[0] if known else len(operands) - 1, first))
        places.append(place)
    if state is not None:
        operands.append(state)
    if final:
        out_shape = jax.ShapeDtypeStruct((SENT_ROWS, WIDTH), jnp.bfloat16)
    else:
        out_shape = jax.ShapeDtypeStruct((HEADS_HERE, ROWS, 3 * HEAD), jnp.float32)
    return pl.pallas_call(
        functools.partial(
            attend_kernel,
            places=places,
            resumed=state is not None,
            final=final,
        ),
        in_specs=[whole] * len(operands),
        out_specs=whole,
        out_shape=out_shape,
        compiler_params=pltpu.CompilerParams(vmem_limit_bytes=VMEM),
        cost_estimate=pl.CostEstimate(flops=1, bytes_accessed=1, transcendentals=0),
    )(*operands)


def merge_kernel(*refs):
    *parts, out_ref = refs
    logs = []
    for part in parts:
        stats = part[ROWS:, :].astype(jnp.float32)
        logs.append(stats[0:8] + (stats[8:16] + stats[16:24]))
    high = functools.reduce(jnp.maximum, logs)
    shares = [jnp.exp2(log - high) for log in logs]
    whole = functools.reduce(jnp.add, shares)
    shares = [share / whole for share in shares]
    eye = diagonal()
    ones = jnp.ones((2 * HEAD, HEAD), jnp.bfloat16)
    for h in range(HEADS_HERE):
        mine = slice(h * HEAD, (h + 1) * HEAD)
        for g in range(ROWS // HEAD):
            at = slice(g * HEAD, (g + 1) * HEAD)
            total = None
            for part, share in zip(parts, shares):
                spread = jnp.where(eye, share[g : g + 1, mine], 0.0)
                coarse = spread.astype(jnp.bfloat16)
                fine = (spread - coarse.astype(jnp.float32)).astype(jnp.bfloat16)
                column = jnp.dot(
                    jnp.concatenate([coarse, fine], axis=1),
                    ones,
                    preferred_element_type=jnp.float32,
                )
                term = part[at, mine].astype(jnp.float32) * column
                total = term if total is None else total + term
            out_ref[at, mine] = total.astype(out_ref.dtype)


def merge(parts):
    return pl.pallas_call(
        merge_kernel,
        in_specs=[pl.BlockSpec(memory_space=pltpu.VMEM)] * len(parts),
        out_specs=pl.BlockSpec(memory_space=pltpu.VMEM),
        out_shape=jax.ShapeDtypeStruct((ROWS, WIDTH), jnp.bfloat16),
        compiler_params=pltpu.CompilerParams(vmem_limit_bytes=VMEM),
        cost_estimate=pl.CostEstimate(flops=1, bytes_accessed=1, transcendentals=0),
    )(*parts)


def swap(array, axis):
    pairs = {"c": [(0, 1)], "xl": [(0, 1)], "y01": [(0, 1), (2, 3)], "y12": [(1, 2), (3, 0)]}[axis]
    both = pairs + [(j, i) for i, j in pairs]
    return lax.ppermute(array, axis[0] if axis[0] == "y" else axis, both)


def after(first, *rest):
    return lax.optimization_barrier((first, *rest))


def per_device(queries, key_states, value_states):
    grouped_kv = regroup(key_states[0], value_states[0])
    own_kv = lax.all_to_all(grouped_kv, ULY, 0, 0).reshape(ROWS, 2 * WIDTH)
    own_kv, queries = after(own_kv, queries)
    next_kv = swap(own_kv, "y01")
    side_kv = swap(own_kv, "y12")
    core_kv = swap(own_kv, "c")
    both_q = lax.all_to_all(copy_out(queries[0]), ("z", "xh", "xl"), 0, 0)
    own_q, far_q = part(both_q)

    def whole(array):
        return (array, 0, array, WIDTH)

    near = [whole(own_kv), whole(core_kv)]
    state_far = attend(far_q, near)
    side_kv, next_kv, state_far = after(side_kv, next_kv, state_far)
    side_core_kv = swap(side_kv, "c")
    next_core_kv = swap(next_kv, "c")
    diagonal_k = swap(next_kv[:, :WIDTH], "y12")
    diagonal_v = swap(side_kv[:, WIDTH:], "y01")

    around = [whole(side_kv), whole(side_core_kv), whole(next_kv), whole(next_core_kv)]
    state_far = attend(far_q, around, state_far)
    state_far, own_q = after(state_far, own_q)
    state_own = attend(own_q, near)
    state_own, state_far, diagonal_k, diagonal_v = after(
        state_own, state_far, diagonal_k, diagonal_v
    )
    diagonal_core_k = swap(diagonal_k, "c")
    diagonal_core_v = swap(diagonal_v, "c")
    diagonal = (diagonal_k, 0, diagonal_v, 0)
    diagonal_core = (diagonal_core_k, 0, diagonal_core_v, 0)
    state_far = attend(far_q, [diagonal], state_far)
    back = swap(attend(far_q, [diagonal_core], state_far, final=True), "xl")
    mine = attend(own_q, around + [diagonal, diagonal_core], state_own, final=True)

    merged = merge([mine, back]).reshape(GROUPS, TOKENS, WIDTH)
    return ungroup(lax.all_to_all(merged, ULY, 0, 0))[None]


def solution(mesh):
    split = Mesh(mesh.devices.reshape(4, 2, 2, 4, 2), ("z", "xh", "xl", "y", "c"))
    placed = P(None, ("z", "xh", "xl", "y", "c"), None)
    return jax.shard_map(
        per_device,
        mesh=split,
        in_specs=(placed, placed, placed),
        out_specs=placed,
        check_vma=False,
    )
```

profile of v0, /device:TPU:0, one launch (start us, length us, event | category | flops | bytes accessed | tf_op | source)
XLA Modules:
  0.0 131.9 jit_solution(7683823811167030681)
XLA Ops:
  0.0 0.0 copy-start.1
  0.0 1.1 copy-done.1
  1.1 0.0 copy-start.2
  1.1 1.1 copy-done.2
  2.1 0.4 shard_map.37
  2.5 0.0 copy-start
  2.5 26.5 %all_to_all.15 = bf16[8,96,768]{2,1,0:T(8,128)(2,1)S(1)} all-to-all(bf16[8,96,768]{2,1,0:T(8,128)(2,1)S(1)} %shard_map.37), channel_id=1, replica_groups=mesh['z'=4,'xh'=2,'xl'=2,'y'=4,'c'=2] {'z','xh'}, dimensions={0} | all-to-all | bytes 2359296 | tf_op jit(solution)/shard_map/all_to_all | solution.py:276
  29.0 0.0 collective-permute-start.2
  29.0 3.0 %collective-permute-start = (bf16[768,768]{1,0:T(8,128)(2,1)S(1)}, bf16[768,768]{1,0:T(8,128)(2,1)S(1)}, u32[]{:S(2)}, u32[]{:S(2)}) collective-permute-start(bf16[768,768]{1,0:T(8,128)(2,1)S(1)} %bitcast.7), channel_id=1, source_target_pairs={{2,4},{6,0},{4,2},{0,6},{3,5},{7,1},{5,3},{1,7},{10,12},{14,8},{12... | collective-permute-start | bytes 3538952 | tf_op jit(solution)/shard_map/ppermute | solution.py:267
  32.0 0.1 collective-permute-start.1
  32.2 0.0 copy-done
  32.2 0.2 shard_map.38
  32.4 21.7 %all_to_all.16.in_ref = bf16[16,96,384]{2,1,0:T(8,128)(2,1)S(1)} all-to-all(bf16[16,96,384]{2,1,0:T(8,128)(2,1)S(1)} %shard_map.38), channel_id=1, replica_groups=mesh['z'=4,'xh'=2,'xl'=2,'y'=4,'c'=2] {'z','xh','xl'}, dimensions={0} | all-to-all | bytes 2359296 | tf_op jit(solution)/shard_map/all_to_all | solution.py:281
  54.1 0.1 shard_map.39
  54.2 0.0 collective-permute-done.2.refs_2_
  54.2 4.6 %shard_map.40.refs_5_ = f32[3,768,384]{2,1,0:T(8,128)S(1)} custom-call(bf16[768,384]{1,0:T(8,128)(2,1)S(1)} %get-tuple-element.19.refs_0_, bf16[768,768]{1,0:T(8,128)(2,1)S(1)} %bitcast.9, bf16[768,768]{1,0:T(8,128)(2,1)S(1)} %collective-permute-done.2.refs_2_), custom_call_target="tpu_custom_call" | custom-call | flops 1 | bytes 1 | tf_op jit(solution)/shard_map/pallas_call | solution.py:207
  58.8 0.0 collective-permute-done.refs_1_
  58.8 1.3 %collective-permute-done.1.refs_3_ = bf16[768,768]{1,0:T(8,128)(2,1)S(1)} collective-permute-done((bf16[768,768]{1,0:T(8,128)(2,1)S(1)}, bf16[768,768]{1,0:T(8,128)(2,1)S(1)}, u32[]{:S(2)}, u32[]{:S(2)}) %collective-permute-start.1) | collective-permute-done | bytes 1179680 | tf_op jit(solution)/shard_map/ppermute | solution.py:267
  60.1 0.0 collective-permute-start.3
  60.1 0.5 collective-permute-start.4
  60.6 0.1 slice.6
  60.7 0.1 slice.7
  60.8 1.6 %collective-permute-start.5 = (bf16[768,384]{1,0:T(8,128)(2,1)S(1)}, bf16[768,384]{1,0:T(8,128)(2,1)S(1)}, u32[]{:S(2)}, u32[]{:S(2)}) collective-permute-start(bf16[768,384]{1,0:T(8,128)(2,1)S(1)} %slice.6), channel_id=1, source_target_pairs={{2,4},{6,0},{4,2},{0,6},{3,5},{7,1},{5,3},{1,7},{10,12},{14,8},{12... | collective-permute-start | bytes 1769480 | tf_op jit(solution)/shard_map/ppermute | solution.py:267
  62.4 0.2 collective-permute-start.6
  62.6 0.4 collective-permute-done.3.refs_2_
  63.0 1.7 %collective-permute-done.4.refs_4_ = bf16[768,768]{1,0:T(8,128)(2,1)S(1)} collective-permute-done((bf16[768,768]{1,0:T(8,128)(2,1)S(1)}, bf16[768,768]{1,0:T(8,128)(2,1)S(1)}, u32[]{:S(2)}, u32[]{:S(2)}) %collective-permute-start.4) | collective-permute-done | bytes 1179680 | tf_op jit(solution)/shard_map/ppermute | solution.py:267
  64.7 9.7 %shard_map.41.refs_3_ = f32[3,768,384]{2,1,0:T(8,128)S(1)} custom-call(bf16[768,384]{1,0:T(8,128)(2,1)S(1)} %get-tuple-element.19.refs_0_, bf16[768,768]{1,0:T(8,128)(2,1)S(1)} %collective-permute-done.refs_1_, bf16[768,768]{1,0:T(8,128)(2,1)S(1)} %collective-permute-done.3.refs_2_, bf16[768,768]{1,0:T(8,128)(2,1)S(1)} %collective-permute-done.1.refs_3_, ...), custom_call_target="tpu_custom_call" | custom-call | flops 1 | bytes 1 | tf_op jit(solution)/shard_map/pallas_call | solution.py:207
  74.4 19.3 %shard_map.42.refs_9_ = f32[3,768,384]{2,1,0:T(8,128)S(1)} custom-call(bf16[768,384]{1,0:T(8,128)(2,1)S(1)} %get-tuple-element.25.refs_0_, bf16[768,768]{1,0:T(8,128)(2,1)S(1)} %bitcast.10, bf16[768,768]{1,0:T(8,128)(2,1)S(1)} %collective-permute-done.2.refs_2_), custom_call_target="tpu_custom_call" | custom-call | flops 1 | bytes 1 | tf_op jit(solution)/shard_map/pallas_call | solution.py:207
  93.7 0.0 collective-permute-done.5.refs_5_.refs_1_
  93.7 0.0 collective-permute-done.6.refs_6_.refs_2_
  93.7 0.2 collective-permute-start.7
  94.0 0.4 collective-permute-start.8
  94.3 2.6 %shard_map.44.refs_3_ = f32[3,768,384]{2,1,0:T(8,128)S(1)} custom-call(bf16[768,384]{1,0:T(8,128)(2,1)S(1)} %get-tuple-element.19.refs_0_, bf16[768,384]{1,0:T(8,128)(2,1)S(1)} %collective-permute-done.5.refs_5_.refs_1_, bf16[768,384]{1,0:T(8,128)(2,1)S(1)} %collective-permute-done.6.refs_6_.refs_2_, f32[3,768,384]{2,1,0:T(8,128)S(1)} %shard_map.41.refs_3_), custom_call_target="tpu_custom_call" | custom-call | flops 1 | bytes 1 | tf_op jit(solution)/shard_map/pallas_call | solution.py:207
  96.9 0.0 collective-permute-done.7.refs_7_.refs_1_
  96.9 0.0 collective-permute-done.8.refs_8_.refs_2_
  96.9 2.5 %shard_map.45 = bf16[800,384]{1,0:T(8,128)(2,1)S(1)} custom-call(bf16[768,384]{1,0:T(8,128)(2,1)S(1)} %get-tuple-element.19.refs_0_, bf16[768,384]{1,0:T(8,128)(2,1)S(1)} %collective-permute-done.7.refs_7_.refs_1_, bf16[768,384]{1,0:T(8,128)(2,1)S(1)} %collective-permute-done.8.refs_8_.refs_2_, f32[3,768,384]{2,1,0:T(8,128)S(1)} %shard_map.44.refs_3_), custom_call_target="tpu_custom_call" | custom-call | flops 1 | bytes 1 | tf_op jit(solution)/shard_map/pallas_call | solution.py:207
  99.5 0.7 collective-permute-start.9
  100.1 14.4 %shard_map.43.refs_0_ = bf16[800,384]{1,0:T(8,128)(2,1)S(1)} custom-call(bf16[768,384]{1,0:T(8,128)(2,1)S(1)} %get-tuple-element.25.refs_0_, bf16[768,768]{1,0:T(8,128)(2,1)S(1)} %collective-permute-done.refs_1_, bf16[768,768]{1,0:T(8,128)(2,1)S(1)} %collective-permute-done.3.refs_2_, bf16[768,768]{1,0:T(8,128)(2,1)S(1)} %collective-permute-done.1.refs_3_, ...), custom_call_target="tpu_custom_call" | custom-call | flops 1 | bytes 1 | tf_op jit(solution)/shard_map/pallas_call | solution.py:207
  114.5 0.9 collective-permute-done.9.refs_1_
  115.4 0.8 shard_map.46
  116.3 14.6 %all_to_all.17.in_ref = bf16[8,96,384]{2,1,0:T(8,128)(2,1)S(1)} all-to-all(bf16[8,96,384]{2,1,0:T(8,128)(2,1)S(1)} %bitcast.11), channel_id=1, replica_groups=mesh['z'=4,'xh'=2,'xl'=2,'y'=4,'c'=2] {'z','xh'}, dimensions={0} | all-to-all | bytes 1179648 | tf_op jit(solution)/shard_map/all_to_all | solution.py:311
  130.9 0.9 shard_map.47
Async XLA Ops:
  0.0 1.1 copy-start.1
  1.1 1.1 copy-start.2
  2.5 29.7 %copy-start = (bf16[1,96,3072]{2,1,0:T(8,128)(2,1)S(1)}, bf16[1,96,3072]{2,1,0:T(8,128)(2,1)}, u32[]{:S(2)}) copy-start(bf16[1,96,3072]{2,1,0:T(8,128)(2,1)} %param.3) | copy-start | bytes 1769476
  29.0 25.2 %collective-permute-start.2 = (bf16[768,768]{1,0:T(8,128)(2,1)S(1)}, bf16[768,768]{1,0:T(8,128)(2,1)S(1)}, u32[]{:S(2)}, u32[]{:S(2)}) collective-permute-start(bf16[768,768]{1,0:T(8,128)(2,1)S(1)} %bitcast.6), channel_id=1, source_target_pairs={{0,1},{1,0},{2,3},{3,2},{4,5},{5,4},{6,7},{7,6},{8,9},{9,8},{10,11... | collective-permute-start | bytes 3538952 | tf_op jit(solution)/shard_map/ppermute | solution.py:267
  29.0 29.8 %collective-permute-start = (bf16[768,768]{1,0:T(8,128)(2,1)S(1)}, bf16[768,768]{1,0:T(8,128)(2,1)S(1)}, u32[]{:S(2)}, u32[]{:S(2)}) collective-permute-start(bf16[768,768]{1,0:T(8,128)(2,1)S(1)} %bitcast.7), channel_id=1, source_target_pairs={{2,4},{6,0},{4,2},{0,6},{3,5},{7,1},{5,3},{1,7},{10,12},{14,8},{12... | collective-permute-start | bytes 3538952 | tf_op jit(solution)/shard_map/ppermute | solution.py:267
  32.0 28.1 %collective-permute-start.1 = (bf16[768,768]{1,0:T(8,128)(2,1)S(1)}, bf16[768,768]{1,0:T(8,128)(2,1)S(1)}, u32[]{:S(2)}, u32[]{:S(2)}) collective-permute-start(bf16[768,768]{1,0:T(8,128)(2,1)S(1)} %bitcast.8), channel_id=1, source_target_pairs={{0,2},{4,6},{2,0},{6,4},{1,3},{5,7},{3,1},{7,5},{8,10},{12,14},{10... | collective-permute-start | bytes 3538952 | tf_op jit(solution)/shard_map/ppermute | solution.py:267
  60.1 2.8 %collective-permute-start.3 = (bf16[768,768]{1,0:T(8,128)(2,1)S(1)}, bf16[768,768]{1,0:T(8,128)(2,1)S(1)}, u32[]{:S(2)}, u32[]{:S(2)}) collective-permute-start(bf16[768,768]{1,0:T(8,128)(2,1)S(1)} %collective-permute-done.refs_1_), channel_id=1, source_target_pairs={{0,1},{1,0},{2,3},{3,2},{4,5},{5,4},{6,7},{7,6},{8,9},{9,8},{10,11... | collective-permute-start | bytes 3538952 | tf_op jit(solution)/shard_map/ppermute | solution.py:267
  60.1 4.5 %collective-permute-start.4 = (bf16[768,768]{1,0:T(8,128)(2,1)S(1)}, bf16[768,768]{1,0:T(8,128)(2,1)S(1)}, u32[]{:S(2)}, u32[]{:S(2)}) collective-permute-start(bf16[768,768]{1,0:T(8,128)(2,1)S(1)} %collective-permute-done.1.refs_3_), channel_id=1, source_target_pairs={{0,1},{1,0},{2,3},{3,2},{4,5},{5,4},{6,7},{7,6},{8,9},{9,8},{10,11... | collective-permute-start | bytes 3538952 | tf_op jit(solution)/shard_map/ppermute | solution.py:267
  60.8 32.9 %collective-permute-start.5 = (bf16[768,384]{1,0:T(8,128)(2,1)S(1)}, bf16[768,384]{1,0:T(8,128)(2,1)S(1)}, u32[]{:S(2)}, u32[]{:S(2)}) collective-permute-start(bf16[768,384]{1,0:T(8,128)(2,1)S(1)} %slice.6), channel_id=1, source_target_pairs={{2,4},{6,0},{4,2},{0,6},{3,5},{7,1},{5,3},{1,7},{10,12},{14,8},{12... | collective-permute-start | bytes 1769480 | tf_op jit(solution)/shard_map/ppermute | solution.py:267
  62.4 31.4 %collective-permute-start.6 = (bf16[768,384]{1,0:T(8,128)(2,1)S(1)}, bf16[768,384]{1,0:T(8,128)(2,1)S(1)}, u32[]{:S(2)}, u32[]{:S(2)}) collective-permute-start(bf16[768,384]{1,0:T(8,128)(2,1)S(1)} %slice.7), channel_id=1, source_target_pairs={{0,2},{4,6},{2,0},{6,4},{1,3},{5,7},{3,1},{7,5},{8,10},{12,14},{10... | collective-permute-start | bytes 1769480 | tf_op jit(solution)/shard_map/ppermute | solution.py:267
  93.7 3.2 %collective-permute-start.7 = (bf16[768,384]{1,0:T(8,128)(2,1)S(1)}, bf16[768,384]{1,0:T(8,128)(2,1)S(1)}, u32[]{:S(2)}, u32[]{:S(2)}) collective-permute-start(bf16[768,384]{1,0:T(8,128)(2,1)S(1)} %collective-permute-done.5.refs_5_.refs_1_), channel_id=1, source_target_pairs={{0,1},{1,0},{2,3},{3,2},{4,5},{5,4},{6,7},{7,6},{8,9},{9,8},{10,11... | collective-permute-start | bytes 1769480 | tf_op jit(solution)/shard_map/ppermute | solution.py:267
  94.0 2.9 %collective-permute-start.8 = (bf16[768,384]{1,0:T(8,128)(2,1)S(1)}, bf16[768,384]{1,0:T(8,128)(2,1)S(1)}, u32[]{:S(2)}, u32[]{:S(2)}) collective-permute-start(bf16[768,384]{1,0:T(8,128)(2,1)S(1)} %collective-permute-done.6.refs_6_.refs_2_), channel_id=1, source_target_pairs={{0,1},{1,0},{2,3},{3,2},{4,5},{5,4},{6,7},{7,6},{8,9},{9,8},{10,11... | collective-permute-start | bytes 1769480 | tf_op jit(solution)/shard_map/ppermute | solution.py:267
  99.5 16.0 %collective-permute-start.9 = (bf16[800,384]{1,0:T(8,128)(2,1)S(1)}, bf16[800,384]{1,0:T(8,128)(2,1)S(1)}, u32[]{:S(2)}, u32[]{:S(2)}) collective-permute-start(bf16[800,384]{1,0:T(8,128)(2,1)S(1)} %shard_map.45), channel_id=1, source_target_pairs={{0,8},{8,0},{1,9},{9,1},{2,10},{10,2},{3,11},{11,3},{4,12},{12,4},... | collective-permute-start | bytes 1843208 | tf_op jit(solution)/shard_map/ppermute | solution.py:267
where the time goes:
time: 131 us; the launch traced here: 132 us
  blocking collectives  62.8 us (48%)
  Pallas kernels  55.4 us (42%)
  starting transfers between devices  6.75 us (5%)
  waiting for transfers between devices  4.38 us (3%)
  local copies, waits for them, and re-layouts  2.25 us (2%)
    pallas_call x6, Pallas kernels, attend(): pl.pallas_call(functools.partial(attend_kernel, places=places, resumed=st...  53 us
    all_to_all x1, blocking collectives, per_device(): own_kv = lax.all_to_all(grouped_kv, ULY, 0, 0).reshape(ROWS, 2 * WIDTH)  26.5 us
    all_to_all x1, blocking collectives, per_device(): both_q = lax.all_to_all(copy_out(queries[0]), ('z', 'xh', 'xl'), 0, 0)  21.7 us
    all_to_all x1, blocking collectives, per_device(): return ungroup(lax.all_to_all(merged, ULY, 0, 0))[None]  14.6 us
    ppermute x10, starting transfers between devices, swap(): return lax.ppermute(array, axis[0] if axis[0] == 'y' else axis, both)  6.75 us
    ppermute x10, waiting for transfers between devices, swap(): return lax.ppermute(array, axis[0] if axis[0] == 'y' else axis, both)  4.38 us
  transfers between devices with their start and end apart: 10, of which 4 were waited for; matrix products, arithmetic and copies ran while one was open for 0% of the time, Pallas kernels for 39%

commit v1 on v0

--- a/solution.py
+++ b/solution.py
@@ -21,6 +21,7 @@
 SCALE = math.log2(math.e) / math.sqrt(HEAD)
 ULY = ("z", "xh")
 VMEM = 20 * 2**20
+WHOLE_VMEM = 60 * 2**20
 
 
 def regroup_kernel(*refs):
@@ -46,7 +47,7 @@
         out_shape=jax.ShapeDtypeStruct((GROUPS, TOKENS, len(arrays) * WIDTH), arrays[0].dtype),
         scratch_shapes=[pltpu.VMEM(array.shape, array.dtype) for array in arrays]
         + [pltpu.SemaphoreType.DMA((len(arrays),))],
-        compiler_params=pltpu.CompilerParams(vmem_limit_bytes=VMEM),
+        compiler_params=pltpu.CompilerParams(vmem_limit_bytes=WHOLE_VMEM),
     )(*arrays)
 
 
@@ -293,12 +294,11 @@
     diagonal_v = swap(side_kv[:, WIDTH:], "y01")
 
     around = [whole(side_kv), whole(side_core_kv), whole(next_kv), whole(next_core_kv)]
+    own_q, state_far = after(own_q, state_far)
+    state_own = attend(own_q, near)
+    state_far, state_own = after(state_far, state_own)
     state_far = attend(far_q, around, state_far)
-    state_far, own_q = after(state_far, own_q)
-    state_own = attend(own_q, near)
-    state_own, state_far, diagonal_k, diagonal_v = after(
-        state_own, state_far, diagonal_k, diagonal_v
-    )
+    state_far, diagonal_k, diagonal_v = after(state_far, diagonal_k, diagonal_v)
     diagonal_core_k = swap(diagonal_k, "c")
     diagonal_core_v = swap(diagonal_v, "c")
     diagonal = (diagonal_k, 0, diagonal_v, 0)

time: 131 us -> 128 us (0.977)
  local copies, waits for them, and re-layouts: 2.25 us -> 0.13 us
  Pallas kernels: 55.4 us -> 53.7 us
    pallas_call x6, Pallas kernels: 53 us -> 49.4 us  [attend(): pl.pallas_call(functools.partial(attend_kernel, places=places, resumed=st...]
    unnamed x6 -> x2, local copies, waits for them, and re-layouts: 2.13 us -> 0.01 us
    pallas_call x1, Pallas kernels: 0.36 us -> 2.33 us  [regroup(): pl.pallas_call(regroup_kernel, in_specs=[pl.BlockSpec(memory_space=pl.ANY...]
  transfers between devices with their start and end apart: 10 -> 10, of which waited for: 4 -> 2; matrix products, arithmetic and copies ran while one was open for 0% -> 0% of each run, Pallas kernels for 39% -> 37%
where the time goes in v1:
time: 128 us
  blocking collectives  62.9 us (49%)
  Pallas kernels  53.7 us (42%)
  starting transfers between devices  6.74 us (5%)
  waiting for transfers between devices  4.15 us (3%)
    pallas_call x6, Pallas kernels, attend(): pl.pallas_call(functools.partial(attend_kernel, places=places, resumed=st...  49.4 us
    all_to_all x1, blocking collectives, per_device(): own_kv = lax.all_to_all(grouped_kv, ULY, 0, 0).reshape(ROWS, 2 * WIDTH)  26.7 us
    all_to_all x1, blocking collectives, per_device(): both_q = lax.all_to_all(copy_out(queries[0]), ('z', 'xh', 'xl'), 0, 0)  21.7 us
    all_to_all x1, blocking collectives, per_device(): return ungroup(lax.all_to_all(merged, ULY, 0, 0))[None]  14.5 us
    ppermute x10, starting transfers between devices, swap(): return lax.ppermute(array, axis[0] if axis[0] == 'y' else axis, both)  6.74 us
    ppermute x10, waiting for transfers between devices, swap(): return lax.ppermute(array, axis[0] if axis[0] == 'y' else axis, both)  4.15 us
  transfers between devices with their start and end apart: 10, of which 2 were waited for; matrix products, arithmetic and copies ran while one was open for 0% of the time, Pallas kernels for 37%

profile of v1, /device:TPU:0, one launch (start us, length us, event | category | flops | bytes accessed | tf_op | source)
XLA Modules:
  0.0 128.0 jit_solution(17146191092426373262)
XLA Ops:
  0.0 2.3 %shard_map.37 = bf16[8,96,768]{2,1,0:T(8,128)(2,1)} custom-call(bf16[96,3072]{1,0:T(8,128)(2,1)} %bitcast.13, bf16[96,3072]{1,0:T(8,128)(2,1)} %bitcast.14), custom_call_target="tpu_custom_call" | custom-call | tf_op jit(solution)/shard_map/pallas_call | solution.py:43
  2.3 0.0 copy-start
  2.3 26.7 %all_to_all.15 = bf16[8,96,768]{2,1,0:T(8,128)(2,1)S(1)} all-to-all(bf16[8,96,768]{2,1,0:T(8,128)(2,1)} %shard_map.37), channel_id=1, replica_groups=mesh['z'=4,'xh'=2,'xl'=2,'y'=4,'c'=2] {'z','xh'}, dimensions={0} | all-to-all | bytes 2359296 | tf_op jit(solution)/shard_map/all_to_all | solution.py:277
  29.1 0.0 collective-permute-start.2
  29.1 3.0 %collective-permute-start = (bf16[768,768]{1,0:T(8,128)(2,1)S(1)}, bf16[768,768]{1,0:T(8,128)(2,1)S(1)}, u32[]{:S(2)}, u32[]{:S(2)}) collective-permute-start(bf16[768,768]{1,0:T(8,128)(2,1)S(1)} %bitcast.7), channel_id=1, source_target_pairs={{2,4},{6,0},{4,2},{0,6},{3,5},{7,1},{5,3},{1,7},{10,12},{14,8},{12... | collective-permute-start | bytes 3538952 | tf_op jit(solution)/shard_map/ppermute | solution.py:268
  32.1 0.1 collective-permute-start.1
  32.2 0.0 copy-done
  32.2 0.2 shard_map.38
  32.5 21.7 %all_to_all.16.in_ref = bf16[16,96,384]{2,1,0:T(8,128)(2,1)S(1)} all-to-all(bf16[16,96,384]{2,1,0:T(8,128)(2,1)S(1)} %shard_map.38), channel_id=1, replica_groups=mesh['z'=4,'xh'=2,'xl'=2,'y'=4,'c'=2] {'z','xh','xl'}, dimensions={0} | all-to-all | bytes 2359296 | tf_op jit(solution)/shard_map/all_to_all | solution.py:282
  54.2 0.1 shard_map.39
  54.3 0.0 collective-permute-done.2.refs_2_
  54.3 4.6 %shard_map.40.refs_5_ = f32[3,768,384]{2,1,0:T(8,128)S(1)} custom-call(bf16[768,384]{1,0:T(8,128)(2,1)S(1)} %get-tuple-element.22.refs_0_, bf16[768,768]{1,0:T(8,128)(2,1)S(1)} %bitcast.9, bf16[768,768]{1,0:T(8,128)(2,1)S(1)} %collective-permute-done.2.refs_2_), custom_call_target="tpu_custom_call" | custom-call | flops 1 | bytes 1 | tf_op jit(solution)/shard_map/pallas_call | solution.py:208
  58.8 0.0 collective-permute-done.refs_1_
  58.8 1.3 %collective-permute-done.1.refs_3_ = bf16[768,768]{1,0:T(8,128)(2,1)S(1)} collective-permute-done((bf16[768,768]{1,0:T(8,128)(2,1)S(1)}, bf16[768,768]{1,0:T(8,128)(2,1)S(1)}, u32[]{:S(2)}, u32[]{:S(2)}) %collective-permute-start.1) | collective-permute-done | bytes 1179680 | tf_op jit(solution)/shard_map/ppermute | solution.py:268
  60.2 0.0 collective-permute-start.3
  60.2 0.5 collective-permute-start.4
  60.7 0.1 slice.6
  60.8 0.1 slice.7
  60.8 1.6 %collective-permute-start.5 = (bf16[768,384]{1,0:T(8,128)(2,1)S(1)}, bf16[768,384]{1,0:T(8,128)(2,1)S(1)}, u32[]{:S(2)}, u32[]{:S(2)}) collective-permute-start(bf16[768,384]{1,0:T(8,128)(2,1)S(1)} %slice.6), channel_id=1, source_target_pairs={{2,4},{6,0},{4,2},{0,6},{3,5},{7,1},{5,3},{1,7},{10,12},{14,8},{12... | collective-permute-start | bytes 1769480 | tf_op jit(solution)/shard_map/ppermute | solution.py:268
  62.4 0.2 collective-permute-start.6
  62.7 4.6 %shard_map.41.refs_9_ = f32[3,768,384]{2,1,0:T(8,128)S(1)} custom-call(bf16[768,384]{1,0:T(8,128)(2,1)S(1)} %get-tuple-element.24.refs_0_, bf16[768,768]{1,0:T(8,128)(2,1)S(1)} %bitcast.10, bf16[768,768]{1,0:T(8,128)(2,1)S(1)} %collective-permute-done.2.refs_2_), custom_call_target="tpu_custom_call" | custom-call | flops 1 | bytes 1 | tf_op jit(solution)/shard_map/pallas_call | solution.py:208
  67.2 0.0 collective-permute-done.3.refs_2_
  67.2 0.0 collective-permute-done.4.refs_4_
  67.2 22.9 %shard_map.42.refs_3_ = f32[3,768,384]{2,1,0:T(8,128)S(1)} custom-call(bf16[768,384]{1,0:T(8,128)(2,1)S(1)} %get-tuple-element.22.refs_0_, bf16[768,768]{1,0:T(8,128)(2,1)S(1)} %collective-permute-done.refs_1_, bf16[768,768]{1,0:T(8,128)(2,1)S(1)} %collective-permute-done.3.refs_2_, bf16[768,768]{1,0:T(8,128)(2,1)S(1)} %collective-permute-done.1.refs_3_, ...), custom_call_target="tpu_custom_call" | custom-call | flops 1 | bytes 1 | tf_op jit(solution)/shard_map/pallas_call | solution.py:208
  90.2 0.0 collective-permute-done.5.refs_5_.refs_1_
  90.2 0.0 collective-permute-done.6.refs_6_.refs_2_
  90.2 0.1 collective-permute-start.7
  90.3 0.5 collective-permute-start.8
  90.8 2.4 %shard_map.44.refs_3_ = f32[3,768,384]{2,1,0:T(8,128)S(1)} custom-call(bf16[768,384]{1,0:T(8,128)(2,1)S(1)} %get-tuple-element.22.refs_0_, bf16[768,384]{1,0:T(8,128)(2,1)S(1)} %collective-permute-done.5.refs_5_.refs_1_, bf16[768,384]{1,0:T(8,128)(2,1)S(1)} %collective-permute-done.6.refs_6_.refs_2_, f32[3,768,384]{2,1,0:T(8,128)S(1)} %shard_map.42.refs_3_), custom_call_target="tpu_custom_call" | custom-call | flops 1 | bytes 1 | tf_op jit(solution)/shard_map/pallas_call | solution.py:208
  93.2 0.0 collective-permute-done.7.refs_7_.refs_1_
  93.2 0.0 collective-permute-done.8.refs_8_.refs_2_
  93.2 2.5 %shard_map.45 = bf16[800,384]{1,0:T(8,128)(2,1)S(1)} custom-call(bf16[768,384]{1,0:T(8,128)(2,1)S(1)} %get-tuple-element.22.refs_0_, bf16[768,384]{1,0:T(8,128)(2,1)S(1)} %collective-permute-done.7.refs_7_.refs_1_, bf16[768,384]{1,0:T(8,128)(2,1)S(1)} %collective-permute-done.8.refs_8_.refs_2_, f32[3,768,384]{2,1,0:T(8,128)S(1)} %shard_map.44.refs_3_), custom_call_target="tpu_custom_call" | custom-call | flops 1 | bytes 1 | tf_op jit(solution)/shard_map/pallas_call | solution.py:208
  95.7 0.7 collective-permute-start.9
  96.4 12.5 %shard_map.43.refs_0_ = bf16[800,384]{1,0:T(8,128)(2,1)S(1)} custom-call(bf16[768,384]{1,0:T(8,128)(2,1)S(1)} %get-tuple-element.24.refs_0_, bf16[768,768]{1,0:T(8,128)(2,1)S(1)} %collective-permute-done.refs_1_, bf16[768,768]{1,0:T(8,128)(2,1)S(1)} %collective-permute-done.3.refs_2_, bf16[768,768]{1,0:T(8,128)(2,1)S(1)} %collective-permute-done.1.refs_3_, ...), custom_call_target="tpu_custom_call" | custom-call | flops 1 | bytes 1 | tf_op jit(solution)/shard_map/pallas_call | solution.py:208
  108.8 2.8 %collective-permute-done.9.refs_1_ = bf16[800,384]{1,0:T(8,128)(2,1)S(1)} collective-permute-done((bf16[800,384]{1,0:T(8,128)(2,1)S(1)}, bf16[800,384]{1,0:T(8,128)(2,1)S(1)}, u32[]{:S(2)}, u32[]{:S(2)}) %collective-permute-start.9) | collective-permute-done | bytes 614432 | tf_op jit(solution)/shard_map/ppermute | solution.py:268
  111.6 0.8 shard_map.46
  112.4 14.5 %all_to_all.17.in_ref = bf16[8,96,384]{2,1,0:T(8,128)(2,1)S(1)} all-to-all(bf16[8,96,384]{2,1,0:T(8,128)(2,1)S(1)} %bitcast.11), channel_id=1, replica_groups=mesh['z'=4,'xh'=2,'xl'=2,'y'=4,'c'=2] {'z','xh'}, dimensions={0} | all-to-all | bytes 1179648 | tf_op jit(solution)/shard_map/all_to_all | solution.py:311
  126.9 0.9 shard_map.47
Async XLA Ops:
  2.3 29.9 %copy-start = (bf16[1,96,3072]{2,1,0:T(8,128)(2,1)S(1)}, bf16[1,96,3072]{2,1,0:T(8,128)(2,1)}, u32[]{:S(2)}) copy-start(bf16[1,96,3072]{2,1,0:T(8,128)(2,1)} %param.3) | copy-start | bytes 1769476
  29.1 25.2 %collective-permute-start.2 = (bf16[768,768]{1,0:T(8,128)(2,1)S(1)}, bf16[768,768]{1,0:T(8,128)(2,1)S(1)}, u32[]{:S(2)}, u32[]{:S(2)}) collective-permute-start(bf16[768,768]{1,0:T(8,128)(2,1)S(1)} %bitcast.6), channel_id=1, source_target_pairs={{0,1},{1,0},{2,3},{3,2},{4,5},{5,4},{6,7},{7,6},{8,9},{9,8},{10,11... | collective-permute-start | bytes 3538952 | tf_op jit(solution)/shard_map/ppermute | solution.py:268
  29.1 29.8 %collective-permute-start = (bf16[768,768]{1,0:T(8,128)(2,1)S(1)}, bf16[768,768]{1,0:T(8,128)(2,1)S(1)}, u32[]{:S(2)}, u32[]{:S(2)}) collective-permute-start(bf16[768,768]{1,0:T(8,128)(2,1)S(1)} %bitcast.7), channel_id=1, source_target_pairs={{2,4},{6,0},{4,2},{0,6},{3,5},{7,1},{5,3},{1,7},{10,12},{14,8},{12... | collective-permute-start | bytes 3538952 | tf_op jit(solution)/shard_map/ppermute | solution.py:268
  32.1 28.1 %collective-permute-start.1 = (bf16[768,768]{1,0:T(8,128)(2,1)S(1)}, bf16[768,768]{1,0:T(8,128)(2,1)S(1)}, u32[]{:S(2)}, u32[]{:S(2)}) collective-permute-start(bf16[768,768]{1,0:T(8,128)(2,1)S(1)} %bitcast.8), channel_id=1, source_target_pairs={{0,2},{4,6},{2,0},{6,4},{1,3},{5,7},{3,1},{7,5},{8,10},{12,14},{10... | collective-permute-start | bytes 3538952 | tf_op jit(solution)/shard_map/ppermute | solution.py:268
  60.2 7.0 %collective-permute-start.3 = (bf16[768,768]{1,0:T(8,128)(2,1)S(1)}, bf16[768,768]{1,0:T(8,128)(2,1)S(1)}, u32[]{:S(2)}, u32[]{:S(2)}) collective-permute-start(bf16[768,768]{1,0:T(8,128)(2,1)S(1)} %collective-permute-done.refs_1_), channel_id=1, source_target_pairs={{0,1},{1,0},{2,3},{3,2},{4,5},{5,4},{6,7},{7,6},{8,9},{9,8},{10,11... | collective-permute-start | bytes 3538952 | tf_op jit(solution)/shard_map/ppermute | solution.py:268
  60.2 7.0 %collective-permute-start.4 = (bf16[768,768]{1,0:T(8,128)(2,1)S(1)}, bf16[768,768]{1,0:T(8,128)(2,1)S(1)}, u32[]{:S(2)}, u32[]{:S(2)}) collective-permute-start(bf16[768,768]{1,0:T(8,128)(2,1)S(1)} %collective-permute-done.1.refs_3_), channel_id=1, source_target_pairs={{0,1},{1,0},{2,3},{3,2},{4,5},{5,4},{6,7},{7,6},{8,9},{9,8},{10,11... | collective-permute-start | bytes 3538952 | tf_op jit(solution)/shard_map/ppermute | solution.py:268
  60.8 29.4 %collective-permute-start.5 = (bf16[768,384]{1,0:T(8,128)(2,1)S(1)}, bf16[768,384]{1,0:T(8,128)(2,1)S(1)}, u32[]{:S(2)}, u32[]{:S(2)}) collective-permute-start(bf16[768,384]{1,0:T(8,128)(2,1)S(1)} %slice.6), channel_id=1, source_target_pairs={{2,4},{6,0},{4,2},{0,6},{3,5},{7,1},{5,3},{1,7},{10,12},{14,8},{12... | collective-permute-start | bytes 1769480 | tf_op jit(solution)/shard_map/ppermute | solution.py:268
  62.4 27.8 %collective-permute-start.6 = (bf16[768,384]{1,0:T(8,128)(2,1)S(1)}, bf16[768,384]{1,0:T(8,128)(2,1)S(1)}, u32[]{:S(2)}, u32[]{:S(2)}) collective-permute-start(bf16[768,384]{1,0:T(8,128)(2,1)S(1)} %slice.7), channel_id=1, source_target_pairs={{0,2},{4,6},{2,0},{6,4},{1,3},{5,7},{3,1},{7,5},{8,10},{12,14},{10... | collective-permute-start | bytes 1769480 | tf_op jit(solution)/shard_map/ppermute | solution.py:268
  90.2 3.0 %collective-permute-start.7 = (bf16[768,384]{1,0:T(8,128)(2,1)S(1)}, bf16[768,384]{1,0:T(8,128)(2,1)S(1)}, u32[]{:S(2)}, u32[]{:S(2)}) collective-permute-start(bf16[768,384]{1,0:T(8,128)(2,1)S(1)} %collective-permute-done.5.refs_5_.refs_1_), channel_id=1, source_target_pairs={{0,1},{1,0},{2,3},{3,2},{4,5},{5,4},{6,7},{7,6},{8,9},{9,8},{10,11... | collective-permute-start | bytes 1769480 | tf_op jit(solution)/shard_map/ppermute | solution.py:268
  90.3 2.9 %collective-permute-start.8 = (bf16[768,384]{1,0:T(8,128)(2,1)S(1)}, bf16[768,384]{1,0:T(8,128)(2,1)S(1)}, u32[]{:S(2)}, u32[]{:S(2)}) collective-permute-start(bf16[768,384]{1,0:T(8,128)(2,1)S(1)} %collective-permute-done.6.refs_6_.refs_2_), channel_id=1, source_target_pairs={{0,1},{1,0},{2,3},{3,2},{4,5},{5,4},{6,7},{7,6},{8,9},{9,8},{10,11... | collective-permute-start | bytes 1769480 | tf_op jit(solution)/shard_map/ppermute | solution.py:268
  95.7 15.9 %collective-permute-start.9 = (bf16[800,384]{1,0:T(8,128)(2,1)S(1)}, bf16[800,384]{1,0:T(8,128)(2,1)S(1)}, u32[]{:S(2)}, u32[]{:S(2)}) collective-permute-start(bf16[800,384]{1,0:T(8,128)(2,1)S(1)} %shard_map.45), channel_id=1, source_target_pairs={{0,8},{8,0},{1,9},{9,1},{2,10},{10,2},{3,11},{11,3},{4,12},{12,4},... | collective-permute-start | bytes 1843208 | tf_op jit(solution)/shard_map/ppermute | solution.py:268
